TPU v7x, 256 devices: a whole 4x4x8 slice. The times are simulated.
256 devices in a mesh: seq: 32 (over x, z), head: 8 (over y, core).
Axes of the slice: x: 4, y: 4, z: 8, core: 2. Of those that a mesh axis runs over, the one named last changes fastest.
Arguments:
- passage_lengths: int32 [64], replicated, may hold values from 1 to 768, 24512 in all
- queries: bfloat16 [24576, 4096], P('seq', 'head'), may hold values from -6 to 6
- keys: bfloat16 [24576, 1024], P('seq', 'head'), may hold values from -6 to 6
- values: bfloat16 [24576, 1024], P('seq', 'head'), may hold values from -6 to 6
- grad_out: bfloat16 [24576, 4096], P('seq', 'head'), may hold values from -0.5 to 0.5
- out_weight: bfloat16 [4096, 4096], P('head'), may hold values from -1.5 to 1.5
Outputs:
- grad_q: bfloat16 [24576, 4096], P('seq', 'head')
- grad_k: bfloat16 [24576, 1024], P('seq', 'head')
- grad_v: bfloat16 [24576, 1024], P('seq', 'head')
- grad_wo: bfloat16 [4096, 4096], P('head', 'seq')
Inputs may be any that keep to these rules, and one draw needn't show every extreme that they name: `passage_lengths`: passage lengths in pack order; they sum to 24512, and the longest is exactly 768.
All inputs are finite; a program needn't handle non-finite values.
Results may differ from a plain program's by a relative error of at most 0.01.
Values may be sent and summed in bfloat16 or wider, within the bound.
A program may use at most 192 MiB of HBM per device.

v0:
```python
import jax
import jax.numpy as jnp
from jax import lax
from jax.sharding import PartitionSpec as P

HEAD_SIZE = 128
ANSWER_TOKENS = 64


def from_root(block, axis, source):
    block = jnp.where(lax.axis_index(axis) == source, block, jnp.zeros_like(block))
    return lax.psum(block, axis)


def from_behind(value, axis, steps):
    count = lax.axis_size(axis)
    first, last = (max(0, -steps), min(count, count - steps))
    return lax.ppermute(value, axis, [(source, source + steps) for source in range(first, last)])


def segment_of(positions, starts):
    hits = (starts[None, :] <= positions[:, None]).astype(jnp.int32)
    return jnp.sum(hits, axis=1) - 1


def contract(left, right, left_dim, right_dim):
    return lax.dot_general(
        left, right, (((left_dim,), (right_dim,)), ((), ())), preferred_element_type=jnp.float32
    )


def on_device(passage_lengths, queries, keys, values, grad_out, out_weight):
    seq_count = lax.axis_size("seq")
    seq_index = lax.axis_index("seq")
    rows = queries.shape[0]
    q_heads = queries.shape[1] // HEAD_SIZE
    kv_heads = keys.shape[1] // HEAD_SIZE
    query_group = q_heads // kv_heads
    scale = HEAD_SIZE ** (-0.5)
    final = seq_count - 1
    answer_start_index = rows * seq_count - ANSWER_TOKENS
    starts = jnp.cumsum(passage_lengths) - passage_lengths
    own_pos = seq_index * rows + jnp.arange(rows, dtype=jnp.int32)
    prior_pos = own_pos - rows
    own_seg = segment_of(own_pos, starts)
    prior_seg = segment_of(prior_pos, starts)
    row_answer = own_pos >= answer_start_index
    answer_query = from_root(queries[rows - ANSWER_TOKENS :], "seq", final)
    whole_grad = lax.all_gather(grad_out, "head", axis=1, tiled=True)
    attention_gradient = contract(whole_grad, out_weight, 1, 1).astype(jnp.bfloat16)
    answer_grad = from_root(attention_gradient[rows - ANSWER_TOKENS :], "seq", final)
    prior_keys, prior_values = from_behind((keys, values), "seq", 1)
    window_keys = jnp.concatenate([prior_keys, keys], axis=0)
    window_values = jnp.concatenate([prior_values, values], axis=0)
    window_pos = jnp.concatenate([prior_pos, own_pos])
    window_seg = jnp.concatenate([prior_seg, own_seg])
    local_mask = (
        (window_pos[None, :] <= own_pos[:, None])
        & (window_seg[None, :] == own_seg[:, None])
        & (~row_answer)[:, None]
    )
    answer_pos = answer_start_index + jnp.arange(ANSWER_TOKENS, dtype=jnp.int32)
    answer_mask = own_pos[None, :] <= answer_pos[:, None]
    answer_flag = row_answer.astype(jnp.float32)
    out_parts = []
    dq_parts = []
    dk_window = [jnp.zeros((2 * rows, HEAD_SIZE), jnp.float32)]
    dv_window = [jnp.zeros((2 * rows, HEAD_SIZE), jnp.float32)]
    answer_scores = []
    answer_tops = []
    answer_masses = []
    for head in range(q_heads):
        kv_head = head // query_group
        q_cols = slice(head * HEAD_SIZE, (head + 1) * HEAD_SIZE)
        head_q = queries[:, q_cols]
        head_g = attention_gradient[:, q_cols]
        score = contract(head_q, window_keys, 1, 1) * scale
        top = jnp.max(jnp.where(local_mask, score, -jnp.inf), axis=1)
        top = jnp.where(row_answer, 0.0, top)
        mass = (
            jnp.sum(jnp.where(local_mask, jnp.exp(score - top[:, None]), 0.0), axis=1) + answer_flag
        )
        lse = top + jnp.log(mass)
        prob = jnp.where(local_mask, jnp.exp(score - lse[:, None]), 0.0)
        prob_low = prob.astype(jnp.bfloat16)
        head_out = jnp.dot(prob_low, window_values, preferred_element_type=jnp.float32).astype(
            jnp.bfloat16
        )
        delta = jnp.sum(head_g.astype(jnp.float32) * head_out.astype(jnp.float32), axis=1)
        dprob = contract(head_g, window_values, 1, 1)
        dscore = (prob * (dprob - delta[:, None])).astype(jnp.bfloat16)
        dq_parts.append(jnp.dot(dscore, window_keys, preferred_element_type=jnp.float32) * scale)
        dk_window[kv_head] = dk_window[kv_head] + contract(dscore, head_q, 0, 0) * scale
        dv_window[kv_head] = dv_window[kv_head] + contract(prob_low, head_g, 0, 0)
        out_parts.append(head_out)
        a_score = contract(answer_query[:, q_cols], keys, 1, 1) * scale
        a_top = jnp.max(jnp.where(answer_mask, a_score, -jnp.inf), axis=1)
        a_mass = jnp.sum(jnp.where(answer_mask, jnp.exp(a_score - a_top[:, None]), 0.0), axis=1)
        answer_scores.append(a_score)
        answer_tops.append(a_top)
        answer_masses.append(a_mass)
    local_tops = jnp.stack(answer_tops)
    local_masses = jnp.stack(answer_masses)
    global_top = lax.pmax(local_tops, "seq")
    global_mass = lax.psum(local_masses * jnp.exp(local_tops - global_top), "seq")
    answer_lse = global_top + jnp.log(global_mass)
    answer_probs = []
    out_terms = []
    for head in range(q_heads):
        kv_head = head // query_group
        a_prob = jnp.where(
            answer_mask, jnp.exp(answer_scores[head] - answer_lse[head][:, None]), 0.0
        )
        answer_probs.append(a_prob)
        out_terms.append(
            jnp.dot(a_prob.astype(jnp.bfloat16), values, preferred_element_type=jnp.float32)
        )
    answer_out = lax.psum(jnp.concatenate(out_terms, axis=1), "seq").astype(jnp.bfloat16)
    dk_answer = [jnp.zeros((rows, HEAD_SIZE), jnp.float32)]
    dv_answer = [jnp.zeros((rows, HEAD_SIZE), jnp.float32)]
    dq_terms = []
    for head in range(q_heads):
        kv_head = head // query_group
        q_cols = slice(head * HEAD_SIZE, (head + 1) * HEAD_SIZE)
        a_grad = answer_grad[:, q_cols]
        a_prob = answer_probs[head]
        a_delta = jnp.sum(
            a_grad.astype(jnp.float32) * answer_out[:, q_cols].astype(jnp.float32), axis=1
        )
        a_dprob = contract(a_grad, values, 1, 1)
        a_dscore = (a_prob * (a_dprob - a_delta[:, None])).astype(jnp.bfloat16)
        dq_terms.append(jnp.dot(a_dscore, keys, preferred_element_type=jnp.float32) * scale)
        dk_answer[kv_head] = (
            dk_answer[kv_head] + contract(a_dscore, answer_query[:, q_cols], 0, 0) * scale
        )
        dv_answer[kv_head] = dv_answer[kv_head] + contract(
            a_prob.astype(jnp.bfloat16), a_grad, 0, 0
        )
    answer_dq = lax.psum(jnp.concatenate(dq_terms, axis=1).astype(jnp.bfloat16), "seq").astype(
        jnp.float32
    )
    dk_prior = jnp.concatenate([part[:rows] for part in dk_window], axis=1)
    dv_prior = jnp.concatenate([part[:rows] for part in dv_window], axis=1)
    back_keys, back_values = from_behind((dk_prior, dv_prior), "seq", -1)
    grad_k = dk_window[0][rows:] + dk_answer[0] + back_keys
    grad_v = dv_window[0][rows:] + dv_answer[0] + back_values
    width_q = q_heads * HEAD_SIZE
    answer_block = jnp.concatenate(
        [jnp.zeros((rows - ANSWER_TOKENS, width_q), jnp.float32), answer_dq], axis=0
    )
    grad_q = jnp.concatenate(dq_parts, axis=1) + jnp.where(row_answer[:, None], answer_block, 0.0)
    out_block = jnp.concatenate(
        [jnp.zeros((rows - ANSWER_TOKENS, width_q), jnp.bfloat16), answer_out], axis=0
    )
    attn_rows = jnp.where(row_answer[:, None], out_block, jnp.concatenate(out_parts, axis=1))
    weight_term = contract(attn_rows, whole_grad, 0, 0)
    grad_wo = lax.psum_scatter(weight_term, "seq", scatter_dimension=1, tiled=True)
    return (
        grad_q.astype(jnp.bfloat16),
        grad_k.astype(jnp.bfloat16),
        grad_v.astype(jnp.bfloat16),
        grad_wo.astype(jnp.bfloat16),
    )


def solution(mesh):
    placed = (
        P(),
        P("seq", "head"),
        P("seq", "head"),
        P("seq", "head"),
        P("seq", "head"),
        P("head", None),
    )
    return jax.shard_map(
        on_device,
        mesh=mesh,
        in_specs=placed,
        out_specs=(P("seq", "head"), P("seq", "head"), P("seq", "head"), P("head", "seq")),
        check_vma=False,
    )
```

profile of v0, /device:TPU:8, one launch (start us, length us, event | category | flops | bytes accessed | tf_op | source)
XLA Modules:
  0.0 869.6 jit_solution(9456568805764287713)
XLA Ops:
  7.2 0.7 all-gather.2.cloned.1.call-update
  7.9 3.8 collective-permute-start
  11.8 3.8 collective-permute-start.1
  15.6 0.7 copy.36
  16.6 0.7 sub.217
  17.5 1.5 slice_select_fusion.1
  19.0 1.0 constant_dynamic-update-slice_fusion
  19.9 0.5 collective-permute-done.1
  20.5 1.0 constant_dynamic-update-slice_fusion.2
  21.4 2.7 fusion.18
  24.2 0.8 fusion.67
  25.0 0.8 fusion.70
  25.8 2.2 copy-done.26
  28.0 3.7 fusion.21
  31.7 5.0 fusion.15
  36.8 2.2 convolution_convert_fusion.3
  39.0 2.2 convolution_convert_fusion.2
  41.3 2.2 convolution_convert_fusion.1
  43.6 11.8 %all-gather.2.cloned.1.call-done = bf16[768,4096]{1,0:T(8,128)(2,1)} async-done(((bf16[768,512]{1,0:T(8,128)(2,1)}), bf16[768,4096]{1,0:T(8,128)(2,1)}) %all-gather.2.cloned.1.call-update) | async-done | bytes 6291472 | tf_op jit(solution)/shard_map/all_gather | solution.py:49
  55.3 7.4 convolution_convert_fusion
  62.8 0.7 slice_select_fusion
  63.6 6.7 multiply_reduce_fusion.3
  70.3 135.2 %all-reduce.9.cloned.1.call-done = (bf16[64,512]{1,0:T(8,128)(2,1)}, bf16[64,512]{1,0:T(8,128)(2,1)}) async-done(((bf16[64,512]{1,0:T(8,128)(2,1)}, bf16[64,512]{1,0:T(8,128)(2,1)}), (bf16[64,512]{1,0:T(8,128)(2,1)}, bf16[64,512]{1,0:T(8,128)(2,1)})) %all-reduce.9.cloned.1.call-update) | async-done | bytes 131088 | tf_op jit(solution)/shard_map/psum | solution.py:12
  205.5 0.9 convolution_multiply_fusion.4
  206.5 0.9 convolution_multiply_fusion.5
  207.4 0.9 convolution_multiply_fusion.6
  208.3 1.1 fusion.58
  209.4 73.0 %pmax.7 = f32[4,64]{1,0:T(4,128)S(1)} all-reduce(f32[4,64]{1,0:T(4,128)S(1)} %pad_maximum_fusion.2), channel_id=1, replica_groups=mesh['seq'=32,'head'=8] {'seq'}, use_global_device_ids=true, to_apply=%region_20.21 | all-reduce | flops 256 | bytes 2048 | tf_op jit(solution)/shard_map/pmax | solution.py:104
  282.4 0.3 fusion.62
  282.8 69.6 %psum.36 = f32[4,64]{1,0:T(4,128)S(1)} all-reduce(f32[4,64]{1,0:T(4,128)S(1)} %maximum_multiply_fusion), channel_id=1, replica_groups=mesh['seq'=32,'head'=8] {'seq'}, use_global_device_ids=true, to_apply=%region_25.26 | all-reduce | flops 256 | bytes 2048 | tf_op jit(solution)/shard_map/psum | solution.py:105
  353.4 139.7 %all-reduce.10 = bf16[64,512]{1,0:T(8,128)(2,1)S(1)} all-reduce(f32[64,512]{1,0:T(8,128)S(1)} %pad_maximum_fusion), channel_id=1, replica_groups=mesh['seq'=32,'head'=8] {'seq'}, use_global_device_ids=true, to_apply=%region_27.28 | all-reduce | flops 32768 | bytes 196608 | tf_op jit(solution)/shard_map/psum | solution.py:118
  494.8 0.6 pad_maximum_fusion.1
  495.5 9.9 %fusion.49 = f32[512,4096]{1,0:T(8,128)} fusion(bf16[768,4096]{1,0:T(8,128)(2,1)} %all-gather.2.cloned.1.call-done, bf16[768,128]{1,0:T(8,128)(2,1)} %copy-done.13, bf16[768,128]{1,0:T(8,128)(2,1)} %copy-done.12, bf16[768,128]{1,0:T(8,128)(2,1)S(1)} %convolution_convert_fusion.3, bf16[768,128]{1,0:T(8,128)(2,1)} %get-tuple-element.42, ...), kind=kOutput, calls=%fused_computation.101 | convolution fusion | flops 3224764416 | bytes 15532800 | tf_op jit(solution)/shard_map/dot_general | solution.py:27
  505.5 1.1 copy-done.17
  506.6 4.7 fusion.89
  511.4 4.6 convolution_add_fusion.2
  516.0 1.9 convolution_add_fusion.1
  518.0 1.9 convolution_add_fusion
  519.9 0.9 slice.144
  520.8 0.2 copy-done.8
  521.0 3.0 multiply_convert_fusion.3
  524.0 0.8 fusion.75
  524.9 3.0 multiply_convert_fusion.2
  527.9 0.8 convolution_add_fusion.5
  528.7 3.0 multiply_convert_fusion.1
  531.7 0.8 convolution_add_fusion.4
  532.5 3.2 multiply_convert_fusion
  535.7 0.8 fusion.28
  536.5 0.8 slice.142
  537.3 1.3 collective-permute-start.2
  538.6 1.3 collective-permute-start.3
  539.9 0.8 convolution_multiply_fusion
  540.7 0.8 convolution_multiply_fusion.1
  541.6 0.8 convolution_multiply_fusion.2
  542.4 0.8 convolution_multiply_fusion.3
  543.7 0.2 convolution_add_fusion.11
  543.9 0.2 convolution_add_fusion.10
  544.4 0.2 convolution_add_fusion.7
  544.7 83.9 %all-reduce.7.cloned.1.call-done = bf16[64,512]{1,0:T(8,128)(2,1)} async-done(((bf16[64,512]{1,0:T(8,128)(2,1)}), bf16[64,512]{1,0:T(8,128)(2,1)}) %all-reduce.7.cloned.1.call-update) | async-done | bytes 65552 | tf_op jit(solution)/shard_map/psum | solution.py:139
  628.5 1.8 fusion.29
  630.3 1.9 fusion.35
  632.3 2.1 fusion.36
  634.3 226.9 %reduce-scatter.2.cloned.1.call-done = f32[512,128]{1,0:T(8,128)} async-done(((f32[512,4096]{1,0:T(8,128)}), f32[512,128]{1,0:T(8,128)}) %reduce-scatter.2.cloned.1.call-update) | async-done | bytes 262160 | tf_op jit(solution)/shard_map/reduce_scatter | solution.py:157
  861.2 1.6 convert_element_type.198
  (132 shorter events, 4.1 us)
Async XLA Ops:
  7.2 48.2 %all-gather.2.cloned.1.call-start = ((), (), s32[]{:S(2)}) async-start(), calls=%async_computation.1 | async-start | bytes 7077888 | tf_op jit(solution)/shard_map/all_gather | solution.py:49
  7.9 197.6 %all-reduce.9.cloned.1.call-start = ((), (), s32[]{:S(2)}) async-start(), calls=%async_computation.4 | async-start | bytes 262144 | tf_op jit(solution)/shard_map/psum | solution.py:12
  7.9 11.0 %collective-permute-start = (bf16[768,128]{1,0:T(8,128)(2,1)}, bf16[768,128]{1,0:T(8,128)(2,1)S(1)}, u32[]{:S(2)}, u32[]{:S(2)}) collective-permute-start(bf16[768,128]{1,0:T(8,128)(2,1)} %param.8), channel_id=1, source_target_pairs={{0,8},{8,16},{16,24},{24,32},{32,40},{40,48},{48,56},{56,64},{64,7... | collective-permute-start | bytes 589832 | tf_op jit(solution)/shard_map/ppermute | solution.py:18
  11.8 8.7 collective-permute-start.1
  17.3 46.3 %copy-start.24 = (pred[768]{0:T(1024)(128)(4,1)}, pred[768]{0:T(1024)(128)(4,1)S(1)}, u32[]{:S(2)}) copy-start(pred[768]{0:T(1024)(128)(4,1)S(1)} %fusion.120) | copy-start | bytes 2308
  21.4 42.1 %copy-start.14 = (bf16[1536,128]{1,0:T(8,128)(2,1)}, bf16[1536,128]{1,0:T(8,128)(2,1)S(1)}, u32[]{:S(2)}) copy-start(bf16[1536,128]{1,0:T(8,128)(2,1)S(1)} %constant_dynamic-update-slice_fusion.2) | copy-start | bytes 1179652
  21.4 2.8 copy-start.5
  24.2 3.8 copy-start.26
  25.0 16.3 %copy-start = (f32[1536,768]{1,0:T(8,128)}, f32[1536,768]{1,0:T(8,128)S(1)}, u32[]{:S(2)}) copy-start(f32[1536,768]{1,0:T(8,128)S(1)} %fusion.67) | copy-start | bytes 14155780
  25.8 13.3 %copy-start.1 = (f32[1536,768]{1,0:T(8,128)}, f32[1536,768]{1,0:T(8,128)S(1)}, u32[]{:S(2)}) copy-start(f32[1536,768]{1,0:T(8,128)S(1)} %fusion.70) | copy-start | bytes 14155780
  31.7 5.1 copy-start.4
  31.7 31.9 %copy-start.18 = (f32[768]{0:T(1024)}, f32[768]{0:T(1024)S(1)}, u32[]{:S(2)}) copy-start(f32[768]{0:T(1024)S(1)} %fusion.111) | copy-start | bytes 9220
  36.7 2.3 copy-start.22
  36.8 2.3 copy-start.20
  41.3 22.3 %copy-start.12 = (bf16[768,128]{1,0:T(8,128)(2,1)}, bf16[768,128]{1,0:T(8,128)(2,1)S(1)}, u32[]{:S(2)}) copy-start(bf16[768,128]{1,0:T(8,128)(2,1)S(1)} %convolution_convert_fusion.2) | copy-start | bytes 589828
  43.5 20.1 %copy-start.13 = (bf16[768,128]{1,0:T(8,128)(2,1)}, bf16[768,128]{1,0:T(8,128)(2,1)S(1)}, u32[]{:S(2)}) copy-start(bf16[768,128]{1,0:T(8,128)(2,1)S(1)} %convolution_convert_fusion.1) | copy-start | bytes 589828
  62.8 7.6 copy-start.16
  63.5 142.1 %copy-start.3 = (bf16[768,128]{1,0:T(8,128)(2,1)S(1)}, bf16[768,128]{1,0:T(8,128)(2,1)}, u32[]{:S(2)}) copy-start(bf16[768,128]{1,0:T(8,128)(2,1)} %param.8) | copy-start | bytes 589828
  63.5 289.2 %copy-start.2 = (bf16[768,128]{1,0:T(8,128)(2,1)S(1)}, bf16[768,128]{1,0:T(8,128)(2,1)}, u32[]{:S(2)}) copy-start(bf16[768,128]{1,0:T(8,128)(2,1)} %param.9) | copy-start | bytes 589828
  63.5 565.0 %all-reduce.7.cloned.1.call-start = ((), (), s32[]{:S(2)}) async-start(), calls=%async_computation.2 | async-start | bytes 131072 | tf_op jit(solution)/shard_map/psum | solution.py:139
  205.5 287.6 %copy-start.9 = (bf16[64,512]{1,0:T(8,128)(2,1)S(1)}, bf16[64,512]{1,0:T(8,128)(2,1)}, u32[]{:S(2)}) copy-start(bf16[64,512]{1,0:T(8,128)(2,1)} %get-tuple-element.30) | copy-start | bytes 196612
  352.7 152.8 %copy-start.6 = (bf16[64,768]{1,0:T(8,128)(2,1)}, bf16[64,768]{1,0:T(8,128)(2,1)S(1)}, u32[]{:S(2)}) copy-start(bf16[64,768]{1,0:T(8,128)(2,1)S(1)} %get-tuple-element.32) | copy-start | bytes 294916
  495.5 365.7 %reduce-scatter.2.cloned.1.call-start = ((), (), s32[]{:S(2)}) async-start(), calls=%async_computation.3 | async-start | bytes 8650752 | tf_op jit(solution)/shard_map/reduce_scatter | solution.py:157
  505.5 1.1 copy-start.17
  505.5 1.1 copy-start.19
  505.5 1.1 copy-start.25
  506.6 4.7 copy-start.23
  506.6 9.3 %slice-start.2 = ((s8[4718592]{0:T(1024)(128)(4,1)}), s8[4194304]{0:T(1024)(128)(4,1)S(1)}, s32[]{:S(2)}) async-start(s8[4718592]{0:T(1024)(128)(4,1)} %bitcast.168), calls=%async_computation.7 | async-start | bytes 8388608
  511.3 4.6 slice-start.3
  511.3 4.6 copy-start.21
  511.3 6.6 slice-start
  516.0 2.0 slice-start.1
  516.0 5.0 slice-start.6
  517.9 3.1 copy-start.15
  517.9 3.1 slice-start.7
  518.0 3.1 copy-start.30
  518.0 6.9 slice-start.4
  519.9 1.1 copy-start.8
  521.0 3.8 slice-start.5
  524.0 0.8 copy-start.29
  524.9 3.8 copy-start.28
  528.7 3.8 copy-start.27
  537.3 93.0 %collective-permute-start.2 = (f32[768,128]{1,0:T(8,128)}, f32[768,128]{1,0:T(8,128)}, u32[]{:S(2)}, u32[]{:S(2)}) collective-permute-start(f32[768,128]{1,0:T(8,128)} %slice.142), channel_id=1, source_target_pairs={{8,0},{16,8},{24,16},{32,24},{40,32},{48,40},{56,48},{64,56},{72,6... | collective-permute-start | bytes 1179656 | tf_op jit(solution)/shard_map/ppermute | solution.py:18
  538.6 93.7 %collective-permute-start.3 = (f32[768,128]{1,0:T(8,128)}, f32[768,128]{1,0:T(8,128)}, u32[]{:S(2)}, u32[]{:S(2)}) collective-permute-start(f32[768,128]{1,0:T(8,128)} %slice.144), channel_id=1, source_target_pairs={{8,0},{16,8},{24,16},{32,24},{40,32},{48,40},{56,48},{64,56},{72,6... | collective-permute-start | bytes 1179656 | tf_op jit(solution)/shard_map/ppermute | solution.py:18
  541.5 1.7 copy-start.11
  541.5 1.9 copy-start.10
  541.5 2.6 copy-start.7
Sparse Core Ops, SparseCore 0:
  9.8 45.4 all-gather.1
  63.6 141.8 all-reduce.8
  495.6 132.8 all-reduce.6
  632.9 228.2 reduce-scatter.1
where the time goes:
time: 876 us; the launch traced here: 870 us
  waiting for transfers between devices  459 us (52%)
  blocking collectives  282 us (32%)
  matrix products  81.8 us (9%)
  between operations  15 us (2%)
  other arithmetic  13 us (1%)
  starting transfers between devices  10.4 us (1%)
    reduce_scatter x1, waiting for transfers between devices, on_device(): lax.psum_scatter(weight_term, 'seq', scatter_dimension=1, tiled=True)  227 us
    psum x1, blocking collectives, on_device(): lax.psum(jnp.concatenate(out_terms, axis=1), 'seq').astype(jnp.bfloat16)  140 us
    psum x1, waiting for transfers between devices, from_root(): return lax.psum(block, axis)  135 us
    psum x1, waiting for transfers between devices, on_device(): lax.psum(jnp.concatenate(dq_terms, axis=1).astype(jnp.bfloat16), 'seq')  83.9 us
    pmax x1, blocking collectives, on_device(): global_top = lax.pmax(local_tops, 'seq')  73 us
    psum x1, blocking collectives, on_device(): lax.psum(local_masses * jnp.exp(local_tops - global_top), 'seq')  69.6 us
    dot_general x34, matrix products, contract(): lax.dot_general(left, right, (((left_dim,), (right_dim,)), ((), ())), pre...  63.7 us
  transfers between devices with their start and end apart: 8, of which 5 were waited for; matrix products, arithmetic and copies ran while one was open for 9% of the time, Pallas kernels for 0%

commit v1 on v0

v1 whole, which is shorter than its diff:
```python
import functools
import math

import jax
import jax.numpy as jnp
from jax import lax
from jax.experimental import pallas as pl
from jax.experimental.pallas import tpu as pltpu
from jax.sharding import PartitionSpec as P

MESH = pl.DeviceIdType.MESH
F32 = jnp.float32
BF16 = jnp.bfloat16
ROWS = 768
HS = 128
ANS = 64
ANS_START = 24512
SCALE = HS ** (-0.5)
LOG2_SCALE = SCALE * math.log2(math.e)
NEG = -1e30
STAGES = 4
TB = 256
WIN = 1024


def dot(a, b):
    return lax.dot_general(a, b, (((1,), (0,)), ((), ())), preferred_element_type=F32)


def dot_nt(a, b):
    return lax.dot_general(a, b, (((1,), (1,)), ((), ())), preferred_element_type=F32)


def kernel(
    len_ref, q_hbm, k_hbm, v_hbm, g_hbm, w_hbm,
    dq_ref, dk_ref, dv_ref, dwo_ref,
    q, g, kwin, vwin, kt, vt, w, wp, perm, G0, G1, G2, G3, gans, ganst, ot, on, da, dat, daat,
    pbuf, bias, sv, qa, sa, pa, st0, stz, st1, stx, sd0, sdz, sd1, sdx,
    oa, oax, oas, dka, dva, dkv_s, dkv_r, dqa, dqaz, dqas, dqax,
    PW_0, PW_1, PW_2, PW_3, XS_0, XS_1, XS_2, XS_3, R1_0, R1_1, R1_2, R1_3, R2_0, R2_1, R2_2, R2_3, T_0, T_1, T_2, T_3, RZ_0, RZ_1, RZ_2, RZ_3,
    loc, ags, agr, kvs, kvr, ans_s, ans_r, sts, str_, oxs, oxr, dqs, dqr, bks, bkr, rss, rsr, zs, zr,
):
    G = (G0, G1, G2, G3)
    PW = (PW_0, PW_1, PW_2, PW_3)
    XS = (XS_0, XS_1, XS_2, XS_3)
    R1 = (R1_0, R1_1, R1_2, R1_3)
    R2 = (R2_0, R2_1, R2_2, R2_3)
    T = (T_0, T_1, T_2, T_3)
    RZ = (RZ_0, RZ_1, RZ_2, RZ_3)
    s = lax.axis_index("seq")
    hd = lax.axis_index("head")
    x, z = s // 8, s % 8
    y, c = hd // 2, hd % 2
    base = s * ROWS

    def at_seq(x_, z_):
        return (x_ * 8 + z_, hd)

    def at_head(y_, c_):
        return (s, y_ * 2 + c_)

    z_devs = [at_seq(x, (z + d) % 8) for d in range(1, 8)]
    x_devs = [at_seq((x + d) % 4, z) for d in range(1, 4)]
    dev_xp, dev_xm = x_devs[0], x_devs[2]
    dev_yp, dev_ym, dev_sib = at_head((y + 1) % 4, c), at_head((y + 3) % 4, c), at_head(y, 1 - c)
    dev_next, dev_prev = ((s + 1) % 32, hd), ((s + 31) % 32, hd)
    on_col = z == 7
    is_src = s == 31

    sends = []

    def rcopy(src, dst, ss, rs, dev):
        return pltpu.make_async_remote_copy(
            src_ref=src, dst_ref=dst, send_sem=ss, recv_sem=rs, device_id=dev, device_id_type=MESH
        )

    def send(src, dst, ss, rs, dev, cond=None):
        copy = rcopy(src, dst, ss, rs, dev)
        if cond is None:
            copy.start()
        else:
            pl.when(cond)(copy.start)
        sends.append((copy, cond))

    def arrived(dst, ss, rs, dev):
        rcopy(dst, dst, ss, rs, dev).wait_recv()

    own = pl.ds(ROWS, ROWS)
    loads = [
        pltpu.make_async_copy(g_hbm, g, loc.at[0]),
        pltpu.make_async_copy(k_hbm, kwin.at[own], loc.at[1]),
        pltpu.make_async_copy(v_hbm, vwin.at[own], loc.at[2]),
        pltpu.make_async_copy(q_hbm, q, loc.at[3]),
        pltpu.make_async_copy(w_hbm, w, loc.at[4]),
    ]
    for copy in loads:
        copy.start()

    barrier = pltpu.get_barrier_semaphore()
    partners = z_devs + x_devs + [dev_yp, dev_ym, dev_sib, dev_next, dev_prev]
    for dev in partners:
        pl.semaphore_signal(barrier, inc=1, device_id=dev, device_id_type=MESH)

    def feat(p):
        return (
            jnp.left_shift(jnp.bitwise_and(jnp.right_shift(p, 5), 3), 7)
            + jnp.left_shift(jnp.right_shift(p, 7), 5)
            + jnp.bitwise_and(p, 31)
        )

    i0 = lax.broadcasted_iota(jnp.int32, (512, 512), 0)
    i1 = lax.broadcasted_iota(jnp.int32, (512, 512), 1)
    perm[0] = jnp.where(feat(i0) == i1, 1.0, 0.0).astype(BF16)
    perm[1] = jnp.where(feat(i1) == i0, 1.0, 0.0).astype(BF16)

    loads[0].wait()
    for k in range(STAGES):
        G[k][0] = dot_nt(perm[0, 128 * k : 128 * (k + 1), :], g[...]).astype(BF16)
    for copy in loads[1:4]:
        copy.wait()
    pl.semaphore_wait(barrier, len(partners))

    def slab(k, slot, half=None):
        if k == STAGES:
            ref = gans.at[slot]
            return ref if half is None else ref.at[pl.ds(32 * half, 32)]
        ref = G[k].at[slot]
        return ref if half is None else ref.at[pl.ds(64 * half, 64)]

    def ag_own(k):
        send(slab(k, 0), slab(k, 6), ags.at[k, 0], agr.at[k, 0], dev_yp)
        send(slab(k, 0), slab(k, 2), ags.at[k, 1], agr.at[k, 1], dev_ym)
        send(slab(k, 0), slab(k, 1), ags.at[k, 4], agr.at[k, 4], dev_sib)

    def ag_forward(k):
        arrived(slab(k, 6), ags.at[k, 0], agr.at[k, 0], dev_ym)
        send(slab(k, 6, 0), slab(k, 4, 0), ags.at[k, 2], agr.at[k, 2], dev_yp)
        send(slab(k, 6), slab(k, 7), ags.at[k, 5], agr.at[k, 5], dev_sib)
        arrived(slab(k, 2), ags.at[k, 1], agr.at[k, 1], dev_yp)
        send(slab(k, 2, 1), slab(k, 4, 1), ags.at[k, 3], agr.at[k, 3], dev_ym)
        send(slab(k, 2), slab(k, 3), ags.at[k, 6], agr.at[k, 6], dev_sib)

    def ag_far(k):
        arrived(slab(k, 4, 0), ags.at[k, 2], agr.at[k, 2], dev_ym)
        arrived(slab(k, 4, 1), ags.at[k, 3], agr.at[k, 3], dev_yp)
        send(slab(k, 4), slab(k, 5), ags.at[k, 7], agr.at[k, 7], dev_sib)

    def ag_done(k):
        for i, slot in ((4, 1), (5, 7), (6, 3), (7, 5)):
            arrived(slab(k, slot), ags.at[k, i], agr.at[k, i], dev_sib)

    tail = pl.ds(ROWS - ANS, ANS)
    answers = ((q.at[tail], qa), (g.at[tail], gans.at[0]))

    def tree(i, level):
        first, ref = answers[i]
        at = lambda n, src, dev, cond: send(src, ref, ans_s.at[i, n], ans_r.at[i], dev, cond)
        if level == 0:
            for d in range(3):
                at(d, first, x_devs[d], is_src)
        elif level == 1:
            for n, d in ((3, 0), (4, 6), (5, 3)):
                at(n, ref, z_devs[d], on_col)
            at(6, ref, dev_xm, on_col & (x == 0))
        else:
            at(7, ref, z_devs[0], mid & (z != 6))
            at(8, ref, z_devs[6], mid & (z != 0))

    mid = (z == 0) | (z == 3) | (z == 6)
    leaf = jnp.logical_not(on_col | mid)

    def tree_wait(cond):
        for i in range(2):

            @pl.when(cond)
            def _(i=i):
                arrived(answers[i][1], ans_s.at[i, 0], ans_r.at[i], dev_xp)

    tree(0, 0)
    ag_own(0)
    for i in (2, 1, 0):
        for a, ref in enumerate((kwin, vwin)):
            r = pl.ds(TB * i, TB)
            send(ref.at[pl.ds(ROWS + TB * i, TB)], ref.at[r], kvs.at[a, i], kvr.at[a, i], dev_next)
    tree(1, 0)
    ag_own(1)

    eye = jnp.where(
        lax.broadcasted_iota(jnp.int32, (HS, HS), 0) == lax.broadcasted_iota(jnp.int32, (HS, HS), 1),
        1.0, 0.0,
    ).astype(BF16)

    def flip(lo, n):
        kt[:, lo : lo + n] = dot_nt(eye, kwin[lo : lo + n, :]).astype(BF16)
        vt[:, lo : lo + n] = dot_nt(eye, vwin[lo : lo + n, :]).astype(BF16)

    flip(ROWS, ROWS)
    pos = base + lax.broadcasted_iota(jnp.int32, (1, ROWS), 1)

    def add_passage(i, carry):
        begin, best = carry
        best = jnp.where(pos >= begin, begin, best)
        return begin + len_ref[i], best

    _, best = lax.fori_loop(0, 64, add_passage, (jnp.int32(0), jnp.zeros((1, ROWS), jnp.int32)))
    sv[0:1, :] = best
    dka[...] = jnp.zeros_like(dka)
    dva[...] = jnp.zeros_like(dva)
    loads[4].wait()

    def permute_w(slot, carry):
        chunk = 2 * ((y + slot // 2) % 4) + (c + slot % 2) % 2
        r = dot(w[:, pl.ds(pl.multiple_of(chunk * 512, 512), 512)], perm[1]).astype(BF16)
        for k in range(STAGES):
            wp[k, :, pl.ds(pl.multiple_of(slot * 128, 128), 128)] = r[:, 128 * k : 128 * (k + 1)]
        return carry

    lax.fori_loop(0, 4, permute_w, 0)
    tree_wait(on_col)
    tree(0, 1)
    tree(1, 1)
    lax.fori_loop(4, 8, permute_w, 0)

    def forward(i):
        for a, ref in enumerate((kwin, vwin)):
            arrived(ref.at[pl.ds(TB * i, TB)], kvs.at[a, i], kvr.at[a, i], dev_prev)
        flip(TB * i, TB)
        u0 = TB * i
        row = lax.broadcasted_iota(jnp.int32, (WIN, TB), 0)
        col = lax.broadcasted_iota(jnp.int32, (WIN, TB), 1)
        low = sv[0:1, u0 : u0 + TB] - (base - ROWS + u0)
        bias[...] = jnp.where((row >= low) & (row <= col + ROWS), 0.0, NEG)
        tpos = base + u0 + lax.broadcasted_iota(jnp.int32, (1, TB), 1)

        def head(h, carry):
            cols = pl.ds(pl.multiple_of(h * HS, HS), HS)
            sc = dot_nt(kwin[u0 : u0 + WIN, :], q[u0 : u0 + TB, cols]) * LOG2_SCALE + bias[...]
            top = jnp.max(sc, axis=0, keepdims=True)
            p = jnp.exp2(sc - top)
            total = jnp.sum(p, axis=0, keepdims=True)
            inv = jnp.where(tpos >= ANS_START, 0.0, 1.0 / total)
            pn = (p * inv).astype(BF16)
            pbuf[i * 4 + h] = pn
            out = dot(vt[:, u0 : u0 + WIN], pn)
            ot[cols, u0 : u0 + TB] = out.astype(BF16)
            on[u0 : u0 + TB, cols] = out.T.astype(BF16)
            return carry

        lax.fori_loop(0, 4, head, 0)

    tree_wait(mid)
    tree(0, 2)
    tree(1, 2)
    ag_forward(0)
    ag_own(2)
    forward(2)
    tree_wait(leaf)
    ag_own(STAGES)
    ag_forward(1)
    ag_far(0)
    ag_own(3)
    forward(1)

    st0[...] = jnp.zeros_like(st0)
    upos = base + lax.broadcasted_iota(jnp.int32, (ROWS, ANS), 0)
    apos = ANS_START + lax.broadcasted_iota(jnp.int32, (ROWS, ANS), 1)
    abias = jnp.where(upos <= apos, 0.0, NEG)
    for h in range(4):
        sc = dot_nt(kwin[ROWS:, :], qa[:, HS * h : HS * (h + 1)]) * LOG2_SCALE + abias
        sa[h] = sc
        top = jnp.max(sc, axis=0, keepdims=True)
        st0[h : h + 1, 0:ANS] = top
        st0[4 + h : 5 + h, 0:ANS] = jnp.sum(jnp.exp2(sc - top), axis=0, keepdims=True)

    def share(src, dst, devs, sem):
        for d, dev in enumerate(devs):
            send(src, dst.at[d], sts.at[sem, d], str_.at[sem, d], dev)

    def shared(dst, devs, sem):
        for d, dev in enumerate(devs):
            arrived(dst.at[d], sts.at[sem, d], str_.at[sem, d], dev)

    def merged(mine, ref, count):
        tiles = [mine[...]] + [ref[i] for i in range(count)]
        top = functools.reduce(jnp.maximum, [tile[0:4, :] for tile in tiles])
        return top, sum(tile[4:8, :] * jnp.exp2(tile[0:4, :] - top) for tile in tiles)

    share(st0, stz, z_devs, 0)
    ag_forward(STAGES)
    ag_far(1)
    forward(0)
    shared(stz, z_devs, 0)
    top, total = merged(st0, stz, 7)
    st1[0:4, :] = top
    st1[4:8, :] = total
    share(st1, stx, x_devs, 1)
    ag_forward(2)

    def half_of(k, xr, half):
        slot = 2 * ((x + xr + 4 - y) % 4) + (half + c) % 2
        return G[k][slot]

    def partial(k, xr):
        rows = jnp.concatenate([half_of(k, xr, 0), half_of(k, xr, 1)], axis=0)
        PW[k][xr] = dot(rows, on[...]).astype(BF16).reshape(8, 32, 512)

    lo, hi = pl.ds(0, 4), pl.ds(4, 4)

    def rs_start(k):
        partial(k, 2)
        send(PW[k].at[2, lo], R1[k].at[0], rss.at[k, 0], rsr.at[k, 0], dev_xp)
        send(PW[k].at[2, hi], R1[k].at[1], rss.at[k, 1], rsr.at[k, 1], dev_xm)
        partial(k, 1)
        send(PW[k].at[1, hi], R2[k].at[0, hi], rss.at[k, 2], rsr.at[k, 2], dev_xp)
        partial(k, 3)
        send(PW[k].at[3, lo], R2[k].at[1, lo], rss.at[k, 3], rsr.at[k, 3], dev_xm)
        partial(k, 0)

    def rs_pass(k):
        arrived(R1[k].at[0], rss.at[k, 0], rsr.at[k, 0], dev_xm)
        XS[k][0] = (PW[k][1, 0:4].astype(F32) + R1[k][0].astype(F32)).astype(BF16)
        send(XS[k].at[0], R2[k].at[0, lo], rss.at[k, 4], rsr.at[k, 4], dev_xp)
        arrived(R1[k].at[1], rss.at[k, 1], rsr.at[k, 1], dev_xp)
        XS[k][1] = (PW[k][3, 4:8].astype(F32) + R1[k][1].astype(F32)).astype(BF16)
        send(XS[k].at[1], R2[k].at[1, hi], rss.at[k, 5], rsr.at[k, 5], dev_xm)

    def rs_merge(k):
        arrived(R2[k].at[0, hi], rss.at[k, 2], rsr.at[k, 2], dev_xm)
        arrived(R2[k].at[1, lo], rss.at[k, 3], rsr.at[k, 3], dev_xp)
        arrived(R2[k].at[0, lo], rss.at[k, 4], rsr.at[k, 4], dev_xm)
        arrived(R2[k].at[1, hi], rss.at[k, 5], rsr.at[k, 5], dev_xp)
        for d in (4, 3, 5, 2, 6, 1, 7, 0):
            zz = (z + d) % 8
            slot = 2 * ((x + 4 - y) % 4) + (zz // 4 + c) % 2
            r = pl.ds(pl.multiple_of(slot * 128 + (zz % 4) * 32, 32), 32)
            term = dot(ganst[k, r, :], oas[...])
            term = term + PW[k][0, zz].astype(F32)
            T[k][d] = (term + R2[k][0, zz].astype(F32) + R2[k][1, zz].astype(F32)).astype(BF16)
            if d:
                send(T[k].at[d], RZ[k].at[d - 1], zs.at[k, d - 1], zr.at[k, d - 1], z_devs[d - 1])

    def rs_end(k):
        total = T[k][0].astype(F32)
        for d in range(7):
            arrived(RZ[k].at[d], zs.at[k, d], zr.at[k, d], z_devs[d])
            total = total + RZ[k][d].astype(F32)
        dwo_ref[:, 32 * k : 32 * (k + 1)] = total.T.astype(BF16)

    def grad_attn(k):
        part = dot(wp[k], G[k][...].reshape(1024, ROWS))
        if k == 0:
            da[...] = part
        elif k < STAGES - 1:
            da[...] = da[...] + part
        else:
            dat[...] = (da[...] + part).astype(BF16)

    ag_done(0)
    rs_start(0)
    shared(stx, x_devs, 1)
    top, total = merged(st1, stx, 3)
    for h in range(4):
        p = jnp.exp2(sa[h] - top[h : h + 1, 0:ANS]) * (1.0 / total[h : h + 1, 0:ANS])
        pn = p.astype(BF16)
        pa[h] = pn
        oa[:, HS * h : HS * (h + 1)] = dot(vt[:, ROWS:], pn).T.astype(BF16)
    for d in range(3):
        send(oa, oax.at[d], oxs.at[d], oxr.at[d], x_devs[d])
    ag_far(STAGES)
    ag_far(2)
    rs_pass(0)
    ag_forward(3)
    ag_done(1)
    rs_start(1)
    grad_attn(0)
    ag_done(STAGES)

    def turn(slot, carry):
        r = dot_nt(perm[0], gans[slot]).astype(BF16)
        for k in range(STAGES):
            ganst[k, pl.ds(pl.multiple_of(slot * 128, 128), 128), :] = r[128 * k : 128 * (k + 1), :]
        return carry

    lax.fori_loop(0, 8, turn, 0)
    rs_pass(1)

    daat[...] = sum(dot(wp[k], ganst[k]) for k in range(STAGES)).astype(BF16)
    sd0[...] = jnp.zeros_like(sd0)
    for h in range(4):
        dp = dot(vwin[ROWS:, :], daat[HS * h : HS * (h + 1), :])
        sd0[h : h + 1, 0:ANS] = jnp.sum(pa[h].astype(F32) * dp, axis=0, keepdims=True)
        sa[h] = dp
    share(sd0, sdz, z_devs, 2)
    ag_far(3)
    for d in range(3):
        arrived(oax.at[d], oxs.at[d], oxr.at[d], x_devs[d])
    oas[...] = (oa[...].astype(F32) + sum(oax[d].astype(F32) for d in range(3))).astype(BF16)
    rs_merge(0)
    ag_done(2)
    rs_start(2)
    grad_attn(1)
    rs_pass(2)
    shared(sdz, z_devs, 2)
    sd1[...] = sd0[...] + sum(sdz[i] for i in range(7))
    share(sd1, sdx, x_devs, 3)
    rs_merge(1)
    ag_done(3)
    rs_start(3)
    grad_attn(2)
    rs_pass(3)
    grad_attn(3)
    rs_merge(2)

    shared(sdx, x_devs, 3)
    delta_a = sd1[...] + sum(sdx[i] for i in range(3))
    for h in range(4):
        pn = pa[h]
        cols = slice(HS * h, HS * (h + 1))
        ds = (pn.astype(F32) * (sa[h] - delta_a[h : h + 1, 0:ANS])).astype(BF16)
        dqa[:, cols] = (dot(kt[:, ROWS:], ds) * SCALE).T.astype(BF16)
        dka[ROWS:, :] = dka[ROWS:, :] + dot(ds, qa[:, cols])
        dva[ROWS:, :] = dva[ROWS:, :] + dot_nt(pn, daat[cols, :])
    for d in range(7):
        send(dqa, dqaz.at[d], dqs.at[d], dqr.at[d], at_seq(x, 7), z == d)

    def backward(i):
        u0 = TB * i

        def head(h, carry):
            cols = pl.ds(pl.multiple_of(h * HS, HS), HS)
            pn = pbuf[i * 4 + h]
            grad = dat[cols, u0 : u0 + TB]
            dp = dot(vwin[u0 : u0 + WIN, :], grad)
            delta = jnp.sum(grad.astype(F32) * ot[cols, u0 : u0 + TB].astype(F32), axis=0, keepdims=True)
            ds = (pn.astype(F32) * (dp - delta)).astype(BF16)
            dqt = dot(kt[:, u0 : u0 + WIN], ds) * SCALE
            dq_ref[u0 : u0 + TB, cols] = dqt.T.astype(BF16)
            dka[u0 : u0 + WIN, :] = dka[u0 : u0 + WIN, :] + dot(ds, q[u0 : u0 + TB, cols])
            dva[u0 : u0 + WIN, :] = dva[u0 : u0 + WIN, :] + dot_nt(pn, grad)
            return carry

        lax.fori_loop(0, 4, head, 0)
        r = pl.ds(u0, TB)
        dkv_s[0, r] = (dka[r, :] * SCALE).astype(BF16)
        dkv_s[1, r] = dva[r, :].astype(BF16)
        for a in range(2):
            send(dkv_s.at[a, r], dkv_r.at[a, r], bks.at[a, i], bkr.at[a, i], dev_prev)

    backward(0)

    @pl.when(on_col)
    def _():
        total = dqa[...].astype(F32)
        for d in range(7):
            arrived(dqaz.at[d], dqs.at[d], dqr.at[d], dev_xp)
            total = total + dqaz[d].astype(F32)
        dqas[...] = total.astype(BF16)

    for d in range(3):
        send(dqas, dqax.at[d], dqs.at[7 + d], dqr.at[7 + d], at_seq(3, 7), on_col & (x == d))
    rs_merge(3)
    backward(1)
    rs_end(0)
    rs_end(1)
    backward(2)

    @pl.when(is_src)
    def _():
        total = dqas[...].astype(F32)
        for d in range(3):
            arrived(dqax.at[d], dqs.at[7 + d], dqr.at[7 + d], dev_xp)
            total = total + dqax[d].astype(F32)
        dq_ref[ROWS - ANS :, :] = total.astype(BF16)

    rs_end(2)
    rs_end(3)
    for i in range(3):
        r = pl.ds(TB * i, TB)
        o = pl.ds(ROWS + TB * i, TB)
        for a in range(2):
            arrived(dkv_r.at[a, r], bks.at[a, i], bkr.at[a, i], dev_next)
        dk_ref[r, :] = (dka[o, :] * SCALE + dkv_r[0, r].astype(F32)).astype(BF16)
        dv_ref[r, :] = (dva[o, :] + dkv_r[1, r].astype(F32)).astype(BF16)

    for copy, cond in sends:
        if cond is None:
            copy.wait_send()
        else:
            pl.when(cond)(copy.wait_send)


def on_device(passage_lengths, queries, keys, values, grad_out, out_weight):
    vm = pltpu.VMEM
    dma = pltpu.SemaphoreType.DMA
    scratch = [
        vm((ROWS, 512), BF16),
        vm((ROWS, 512), BF16),
        vm((2 * ROWS, HS), BF16),
        vm((2 * ROWS, HS), BF16),
        vm((HS, 2 * ROWS), BF16),
        vm((HS, 2 * ROWS), BF16),
        vm((512, 4096), BF16),
        vm((STAGES, 512, 1024), BF16),
        vm((2, 512, 512), BF16),
        *[vm((8, 128, ROWS), BF16) for _ in range(STAGES)],
        vm((8, ANS, 512), BF16),
        vm((STAGES, 1024, ANS), BF16),
        vm((512, ROWS), BF16),
        vm((ROWS, 512), BF16),
        vm((512, ROWS), F32),
        vm((512, ROWS), BF16),
        vm((512, ANS), BF16),
        vm((12, WIN, TB), BF16),
        vm((WIN, TB), F32),
        vm((8, ROWS), jnp.int32),
        vm((ANS, 512), BF16),
        vm((4, ROWS, ANS), F32),
        vm((4, ROWS, ANS), BF16),
        vm((8, 128), F32),
        vm((7, 8, 128), F32),
        vm((8, 128), F32),
        vm((3, 8, 128), F32),
        vm((8, 128), F32),
        vm((7, 8, 128), F32),
        vm((8, 128), F32),
        vm((3, 8, 128), F32),
        vm((ANS, 512), BF16),
        vm((3, ANS, 512), BF16),
        vm((ANS, 512), BF16),
        vm((2 * ROWS, HS), F32),
        vm((2 * ROWS, HS), F32),
        vm((2, ROWS, HS), BF16),
        vm((2, ROWS, HS), BF16),
        vm((ANS, 512), BF16),
        vm((7, ANS, 512), BF16),
        vm((ANS, 512), BF16),
        vm((3, ANS, 512), BF16),
        *[vm((4, 8, 32, 512), BF16) for _ in range(STAGES)],
        *[vm((2, 4, 32, 512), BF16) for _ in range(STAGES)],
        *[vm((2, 4, 32, 512), BF16) for _ in range(STAGES)],
        *[vm((2, 8, 32, 512), BF16) for _ in range(STAGES)],
        *[vm((8, 32, 512), BF16) for _ in range(STAGES)],
        *[vm((7, 32, 512), BF16) for _ in range(STAGES)],
        dma((5,)),
        dma((STAGES + 1, 8)),
        dma((STAGES + 1, 8)),
        dma((2, 3)),
        dma((2, 3)),
        dma((2, 9)),
        dma((2,)),
        dma((4, 7)),
        dma((4, 7)),
        dma((3,)),
        dma((3,)),
        dma((10,)),
        dma((10,)),
        dma((2, 3)),
        dma((2, 3)),
        dma((STAGES, 6)),
        dma((STAGES, 6)),
        dma((STAGES, 7)),
        dma((STAGES, 7)),
    ]
    hbm = pl.BlockSpec(memory_space=pl.ANY)
    vmem = pl.BlockSpec(memory_space=pltpu.VMEM)
    return pl.pallas_call(
        kernel,
        out_shape=(
            jax.ShapeDtypeStruct((ROWS, 512), BF16),
            jax.ShapeDtypeStruct((ROWS, HS), BF16),
            jax.ShapeDtypeStruct((ROWS, HS), BF16),
            jax.ShapeDtypeStruct((512, HS), BF16),
        ),
        in_specs=[pl.BlockSpec(memory_space=pltpu.SMEM)] + [hbm] * 5,
        out_specs=(vmem,) * 4,
        scratch_shapes=scratch,
        compiler_params=pltpu.CompilerParams(
            collective_id=0, has_side_effects=True, vmem_limit_bytes=60 * 2**20
        ),
        cost_estimate=pl.CostEstimate(flops=14 * 10**9, bytes_accessed=10**7, transcendentals=4 * 10**6),
    )(passage_lengths, queries, keys, values, grad_out, out_weight)


def solution(mesh):
    placed = (
        P(),
        P("seq", "head"),
        P("seq", "head"),
        P("seq", "head"),
        P("seq", "head"),
        P("head", None),
    )
    return jax.shard_map(
        on_device,
        mesh=mesh,
        in_specs=placed,
        out_specs=(P("seq", "head"), P("seq", "head"), P("seq", "head"), P("head", "seq")),
        check_vma=False,
    )
```

time: 876 us -> 109 us (0.12)
  the two profiles are of different devices: /device:TPU:8 before, /device:TPU:192 now
where the time goes in v1:
time: 109 us
  Pallas kernels  101 us (93%)
  local copies, waits for them, and re-layouts  6.86 us (6%)
    pallas_call x1, Pallas kernels, on_device(): pl.pallas_call(kernel, out_shape=(jax.ShapeDtypeStruct((ROWS, 512), BF16)...  101 us
    unnamed x4, local copies, waits for them, and re-layouts  6.86 us

profile of v1, /device:TPU:192, one launch (start us, length us, event | category | flops | bytes accessed | tf_op | source)
XLA Modules:
  0.0 108.9 jit_solution(18176953861767945592)
XLA Ops:
  0.6 101.4 %shard_map.93 = (bf16[768,512]{1,0:T(8,128)(2,1)}, bf16[768,128]{1,0:T(8,128)(2,1)}, bf16[768,128]{1,0:T(8,128)(2,1)}, bf16[512,128]{1,0:T(8,128)(2,1)}) custom-call(s32[64]{0:T(128)} %len_ref.1, bf16[768,512]{1,0:T(8,128)(2,1)} %q_hbm.1, bf16[768,128]{1,0:T(8,128)(2,1)} %k_hbm.1, bf16[768,128]{1,0:T(8,128)(2,1)} %v_hbm.1, bf16[768,512]{1,0:T(8,128)(2,1)} %g_hbm.1, ...), custom_call_target="tpu_custom_call" | custom-call | flops 14000000000 | bytes 10000000 | tf_op jit(solution)/shard_map/pallas_call | solution.py:566
  102.0 2.1 %copy.14 = bf16[768,512]{1,0:T(8,128)(2,1)} copy(bf16[768,512]{1,0:T(8,128)(2,1)} %get-tuple-element.8) | data formatting | bytes 1572864
  104.1 1.6 %copy.15 = bf16[768,128]{1,0:T(8,128)(2,1)} copy(bf16[768,128]{1,0:T(8,128)(2,1)} %get-tuple-element.9) | data formatting | bytes 393216
  105.7 1.6 %copy.16 = bf16[768,128]{1,0:T(8,128)(2,1)} copy(bf16[768,128]{1,0:T(8,128)(2,1)} %get-tuple-element.10) | data formatting | bytes 393216
  107.3 1.6 %copy.17 = bf16[512,128]{1,0:T(8,128)(2,1)} copy(bf16[512,128]{1,0:T(8,128)(2,1)} %get-tuple-element.11) | data formatting | bytes 262144

commit v2 on v1

--- a/solution.py
+++ b/solution.py
@@ -36,9 +36,9 @@
     dq_ref, dk_ref, dv_ref, dwo_ref,
     q, g, kwin, vwin, kt, vt, w, wp, perm, G0, G1, G2, G3, gans, ganst, ot, on, da, dat, daat,
     pbuf, bias, sv, qa, sa, pa, st0, stz, st1, stx, sd0, sdz, sd1, sdx,
-    oa, oax, oas, dka, dva, dkv_s, dkv_r, dqa, dqaz, dqas, dqax,
+    oa, oax, oas, opd, opr, opc, opg, otot, dka, dva, dkv_s, dkv_r, dqa, dqaz, dqas, dqax,
     PW_0, PW_1, PW_2, PW_3, XS_0, XS_1, XS_2, XS_3, R1_0, R1_1, R1_2, R1_3, R2_0, R2_1, R2_2, R2_3, T_0, T_1, T_2, T_3, RZ_0, RZ_1, RZ_2, RZ_3,
-    loc, ags, agr, kvs, kvr, ans_s, ans_r, sts, str_, oxs, oxr, dqs, dqr, bks, bkr, rss, rsr, zs, zr,
+    loc, ags, agr, kvs, kvr, ans_s, ans_r, sts, str_, oxs, oxr, ops, opq, dqs, dqr, bks, bkr, rss, rsr, zs, zr,
 ):
     G = (G0, G1, G2, G3)
     PW = (PW_0, PW_1, PW_2, PW_3)
@@ -114,8 +114,9 @@
     perm[1] = jnp.where(feat(i1) == i0, 1.0, 0.0).astype(BF16)
 
     loads[0].wait()
+    turned = dot_nt(perm[0], g[...]).astype(BF16)
     for k in range(STAGES):
-        G[k][0] = dot_nt(perm[0, 128 * k : 128 * (k + 1), :], g[...]).astype(BF16)
+        G[k][0] = turned[128 * k : 128 * (k + 1), :]
     for copy in loads[1:4]:
         copy.wait()
     pl.semaphore_wait(barrier, len(partners))
@@ -169,12 +170,10 @@
     mid = (z == 0) | (z == 3) | (z == 6)
     leaf = jnp.logical_not(on_col | mid)
 
-    def tree_wait(cond):
-        for i in range(2):
-
-            @pl.when(cond)
-            def _(i=i):
-                arrived(answers[i][1], ans_s.at[i, 0], ans_r.at[i], dev_xp)
+    def tree_wait(i, cond):
+        @pl.when(cond)
+        def _():
+            arrived(answers[i][1], ans_s.at[i, 0], ans_r.at[i], dev_xp)
 
     tree(0, 0)
     ag_own(0)
@@ -216,10 +215,21 @@
         return carry
 
     lax.fori_loop(0, 4, permute_w, 0)
-    tree_wait(on_col)
+    tree_wait(0, on_col)
     tree(0, 1)
-    tree(1, 1)
-    lax.fori_loop(4, 8, permute_w, 0)
+
+    def share(src, dst, devs, sem):
+        for d, dev in enumerate(devs):
+            send(src, dst.at[d], sts.at[sem, d], str_.at[sem, d], dev)
+
+    def shared(dst, devs, sem):
+        for d, dev in enumerate(devs):
+            arrived(dst.at[d], sts.at[sem, d], str_.at[sem, d], dev)
+
+    def merged(mine, ref, count):
+        tiles = [mine[...]] + [ref[i] for i in range(count)]
+        top = functools.reduce(jnp.maximum, [tile[0:4, :] for tile in tiles])
+        return top, sum(tile[4:8, :] * jnp.exp2(tile[0:4, :] - top) for tile in tiles)
 
     def forward(i):
         for a, ref in enumerate((kwin, vwin)):
@@ -246,20 +256,22 @@
             on[u0 : u0 + TB, cols] = out.T.astype(BF16)
             return carry
 
-        lax.fori_loop(0, 4, head, 0)
-
-    tree_wait(mid)
+        lax.fori_loop(0, 4, head, 0, unroll=True)
+
+    forward(2)
+    tree_wait(0, mid)
     tree(0, 2)
-    tree(1, 2)
+    tree_wait(1, on_col)
+    tree(1, 1)
     ag_forward(0)
     ag_own(2)
-    forward(2)
-    tree_wait(leaf)
-    ag_own(STAGES)
+    forward(1)
+    tree_wait(1, mid)
+    tree(1, 2)
     ag_forward(1)
+    ag_own(3)
     ag_far(0)
-    ag_own(3)
-    forward(1)
+    tree_wait(0, leaf)
 
     st0[...] = jnp.zeros_like(st0)
     upos = base + lax.broadcasted_iota(jnp.int32, (ROWS, ANS), 0)
@@ -272,29 +284,10 @@
         st0[h : h + 1, 0:ANS] = top
         st0[4 + h : 5 + h, 0:ANS] = jnp.sum(jnp.exp2(sc - top), axis=0, keepdims=True)
 
-    def share(src, dst, devs, sem):
-        for d, dev in enumerate(devs):
-            send(src, dst.at[d], sts.at[sem, d], str_.at[sem, d], dev)
-
-    def shared(dst, devs, sem):
-        for d, dev in enumerate(devs):
-            arrived(dst.at[d], sts.at[sem, d], str_.at[sem, d], dev)
-
-    def merged(mine, ref, count):
-        tiles = [mine[...]] + [ref[i] for i in range(count)]
-        top = functools.reduce(jnp.maximum, [tile[0:4, :] for tile in tiles])
-        return top, sum(tile[4:8, :] * jnp.exp2(tile[0:4, :] - top) for tile in tiles)
-
     share(st0, stz, z_devs, 0)
-    ag_forward(STAGES)
-    ag_far(1)
     forward(0)
-    shared(stz, z_devs, 0)
-    top, total = merged(st0, stz, 7)
-    st1[0:4, :] = top
-    st1[4:8, :] = total
-    share(st1, stx, x_devs, 1)
-    ag_forward(2)
+    tree_wait(1, leaf)
+    ag_own(STAGES)
 
     def half_of(k, xr, half):
         slot = 2 * ((x + xr + 4 - y) % 4) + (half + c) % 2
@@ -331,20 +324,50 @@
         arrived(R2[k].at[1, hi], rss.at[k, 5], rsr.at[k, 5], dev_xp)
         for d in (4, 3, 5, 2, 6, 1, 7, 0):
             zz = (z + d) % 8
-            slot = 2 * ((x + 4 - y) % 4) + (zz // 4 + c) % 2
-            r = pl.ds(pl.multiple_of(slot * 128 + (zz % 4) * 32, 32), 32)
-            term = dot(ganst[k, r, :], oas[...])
-            term = term + PW[k][0, zz].astype(F32)
+            term = PW[k][0, zz].astype(F32)
             T[k][d] = (term + R2[k][0, zz].astype(F32) + R2[k][1, zz].astype(F32)).astype(BF16)
             if d:
                 send(T[k].at[d], RZ[k].at[d - 1], zs.at[k, d - 1], zr.at[k, d - 1], z_devs[d - 1])
 
     def rs_end(k):
-        total = T[k][0].astype(F32)
+        slot = 2 * ((x + 4 - y) % 4) + (z // 4 + c) % 2
+        r = pl.ds(pl.multiple_of(slot * 128 + (z % 4) * 32, 32), 32)
+        total = T[k][0].astype(F32) + dot(ganst[k, r, :], otot[...])
         for d in range(7):
             arrived(RZ[k].at[d], zs.at[k, d], zr.at[k, d], z_devs[d])
             total = total + RZ[k][d].astype(F32)
         dwo_ref[:, 32 * k : 32 * (k + 1)] = total.T.astype(BF16)
+
+    def piece(zz):
+        rows = pl.ds(pl.multiple_of(16 * (zz // 2), 16), 16)
+        return rows, pl.ds(pl.multiple_of(256 * (zz % 2), 256), 256)
+
+    def answer_split():
+        for d in range(3):
+            arrived(oax.at[d], oxs.at[d], oxr.at[d], x_devs[d])
+        oas[...] = (oa[...].astype(F32) + sum(oax[d].astype(F32) for d in range(3))).astype(BF16)
+        for d in range(8):
+            rows, cols = piece((z + d) % 8)
+            opd[d] = oas[rows, cols]
+        for d in range(1, 8):
+            send(opd.at[d], opr.at[d - 1], ops.at[0, d - 1], opq.at[0, d - 1], z_devs[d - 1])
+
+    def answer_join():
+        total = opd[0].astype(F32)
+        for d in range(7):
+            arrived(opr.at[d], ops.at[0, d], opq.at[0, d], z_devs[d])
+            total = total + opr[d].astype(F32)
+        opc[...] = total.astype(BF16)
+        for d in range(7):
+            send(opc, opg.at[d], ops.at[1, d], opq.at[1, d], z_devs[d])
+
+    def answer_whole():
+        rows, cols = piece(z)
+        otot[rows, cols] = opc[...]
+        for d in range(7):
+            arrived(opg.at[d], ops.at[1, d], opq.at[1, d], z_devs[d])
+            rows, cols = piece((z + 7 - d) % 8)
+            otot[rows, cols] = opg[d]
 
     def grad_attn(k):
         part = dot(wp[k], G[k][...].reshape(1024, ROWS))
@@ -355,8 +378,15 @@
         else:
             dat[...] = (da[...] + part).astype(BF16)
 
+    shared(stz, z_devs, 0)
+    top, total = merged(st0, stz, 7)
+    st1[0:4, :] = top
+    st1[4:8, :] = total
+    share(st1, stx, x_devs, 1)
     ag_done(0)
     rs_start(0)
+    ag_forward(2)
+    ag_far(1)
     shared(stx, x_devs, 1)
     top, total = merged(st1, stx, 3)
     for h in range(4):
@@ -366,12 +396,21 @@
         oa[:, HS * h : HS * (h + 1)] = dot(vt[:, ROWS:], pn).T.astype(BF16)
     for d in range(3):
         send(oa, oax.at[d], oxs.at[d], oxr.at[d], x_devs[d])
-    ag_far(STAGES)
-    ag_far(2)
+
     rs_pass(0)
-    ag_forward(3)
     ag_done(1)
     rs_start(1)
+    ag_forward(3)
+    ag_far(2)
+    ag_forward(STAGES)
+    lax.fori_loop(4, 8, permute_w, 0)
+    ag_far(3)
+    ag_far(STAGES)
+    rs_pass(1)
+    ag_done(2)
+    rs_start(2)
+    answer_split()
+    rs_merge(0)
     grad_attn(0)
     ag_done(STAGES)
 
@@ -382,7 +421,6 @@
         return carry
 
     lax.fori_loop(0, 8, turn, 0)
-    rs_pass(1)
 
     daat[...] = sum(dot(wp[k], ganst[k]) for k in range(STAGES)).astype(BF16)
     sd0[...] = jnp.zeros_like(sd0)
@@ -391,37 +429,18 @@
         sd0[h : h + 1, 0:ANS] = jnp.sum(pa[h].astype(F32) * dp, axis=0, keepdims=True)
         sa[h] = dp
     share(sd0, sdz, z_devs, 2)
-    ag_far(3)
-    for d in range(3):
-        arrived(oax.at[d], oxs.at[d], oxr.at[d], x_devs[d])
-    oas[...] = (oa[...].astype(F32) + sum(oax[d].astype(F32) for d in range(3))).astype(BF16)
-    rs_merge(0)
-    ag_done(2)
-    rs_start(2)
+    rs_pass(2)
+    ag_done(3)
+    rs_start(3)
+    rs_merge(1)
+    answer_join()
     grad_attn(1)
-    rs_pass(2)
+    grad_attn(2)
+    grad_attn(3)
     shared(sdz, z_devs, 2)
     sd1[...] = sd0[...] + sum(sdz[i] for i in range(7))
     share(sd1, sdx, x_devs, 3)
-    rs_merge(1)
-    ag_done(3)
-    rs_start(3)
-    grad_attn(2)
     rs_pass(3)
-    grad_attn(3)
-    rs_merge(2)
-
-    shared(sdx, x_devs, 3)
-    delta_a = sd1[...] + sum(sdx[i] for i in range(3))
-    for h in range(4):
-        pn = pa[h]
-        cols = slice(HS * h, HS * (h + 1))
-        ds = (pn.astype(F32) * (sa[h] - delta_a[h : h + 1, 0:ANS])).astype(BF16)
-        dqa[:, cols] = (dot(kt[:, ROWS:], ds) * SCALE).T.astype(BF16)
-        dka[ROWS:, :] = dka[ROWS:, :] + dot(ds, qa[:, cols])
-        dva[ROWS:, :] = dva[ROWS:, :] + dot_nt(pn, daat[cols, :])
-    for d in range(7):
-        send(dqa, dqaz.at[d], dqs.at[d], dqr.at[d], at_seq(x, 7), z == d)
 
     def backward(i):
         u0 = TB * i
@@ -439,7 +458,7 @@
             dva[u0 : u0 + WIN, :] = dva[u0 : u0 + WIN, :] + dot_nt(pn, grad)
             return carry
 
-        lax.fori_loop(0, 4, head, 0)
+        lax.fori_loop(0, 4, head, 0, unroll=True)
         r = pl.ds(u0, TB)
         dkv_s[0, r] = (dka[r, :] * SCALE).astype(BF16)
         dkv_s[1, r] = dva[r, :].astype(BF16)
@@ -447,6 +466,25 @@
             send(dkv_s.at[a, r], dkv_r.at[a, r], bks.at[a, i], bkr.at[a, i], dev_prev)
 
     backward(0)
+    rs_merge(2)
+
+    shared(sdx, x_devs, 3)
+    delta_a = sd1[...] + sum(sdx[i] for i in range(3))
+    for h in range(4):
+        pn = pa[h]
+        cols = slice(HS * h, HS * (h + 1))
+        ds = (pn.astype(F32) * (sa[h] - delta_a[h : h + 1, 0:ANS])).astype(BF16)
+        dqa[:, cols] = (dot(kt[:, ROWS:], ds) * SCALE).T.astype(BF16)
+        dka[ROWS:, :] = dka[ROWS:, :] + dot(ds, qa[:, cols])
+        dva[ROWS:, :] = dva[ROWS:, :] + dot_nt(pn, daat[cols, :])
+    for d in range(7):
+        send(dqa, dqaz.at[d], dqs.at[d], dqr.at[d], at_seq(x, 7), z == d)
+
+
+    backward(1)
+
+    rs_merge(3)
+    backward(2)
 
     @pl.when(on_col)
     def _():
@@ -458,19 +496,9 @@
 
     for d in range(3):
         send(dqas, dqax.at[d], dqs.at[7 + d], dqr.at[7 + d], at_seq(3, 7), on_col & (x == d))
-    rs_merge(3)
-    backward(1)
+    answer_whole()
     rs_end(0)
     rs_end(1)
-    backward(2)
-
-    @pl.when(is_src)
-    def _():
-        total = dqas[...].astype(F32)
-        for d in range(3):
-            arrived(dqax.at[d], dqs.at[7 + d], dqr.at[7 + d], dev_xp)
-            total = total + dqax[d].astype(F32)
-        dq_ref[ROWS - ANS :, :] = total.astype(BF16)
 
     rs_end(2)
     rs_end(3)
@@ -482,11 +510,24 @@
         dk_ref[r, :] = (dka[o, :] * SCALE + dkv_r[0, r].astype(F32)).astype(BF16)
         dv_ref[r, :] = (dva[o, :] + dkv_r[1, r].astype(F32)).astype(BF16)
 
+    @pl.when(is_src)
+    def _():
+        total = dqas[...].astype(F32)
+        for d in range(3):
+            arrived(dqax.at[d], dqs.at[7 + d], dqr.at[7 + d], dev_xp)
+            total = total + dqax[d].astype(F32)
+        dq_ref[ROWS - ANS :, :] = total.astype(BF16)
+
     for copy, cond in sends:
         if cond is None:
             copy.wait_send()
         else:
             pl.when(cond)(copy.wait_send)
+
+
+def hand_over(*refs):
+    for i in range(4):
+        refs[4 + i][...] = refs[i][...]
 
 
 def on_device(passage_lengths, queries, keys, values, grad_out, out_weight):
@@ -527,6 +568,11 @@
         vm((ANS, 512), BF16),
         vm((3, ANS, 512), BF16),
         vm((ANS, 512), BF16),
+        vm((8, 16, 256), BF16),
+        vm((7, 16, 256), BF16),
+        vm((16, 256), BF16),
+        vm((7, 16, 256), BF16),
+        vm((ANS, 512), BF16),
         vm((2 * ROWS, HS), F32),
         vm((2 * ROWS, HS), F32),
         vm((2, ROWS, HS), BF16),
@@ -552,6 +598,8 @@
         dma((4, 7)),
         dma((3,)),
         dma((3,)),
+        dma((2, 7)),
+        dma((2, 7)),
         dma((10,)),
         dma((10,)),
         dma((2, 3)),
@@ -563,14 +611,15 @@
     ]
     hbm = pl.BlockSpec(memory_space=pl.ANY)
     vmem = pl.BlockSpec(memory_space=pltpu.VMEM)
-    return pl.pallas_call(
+    out_shape = (
+        jax.ShapeDtypeStruct((ROWS, 512), BF16),
+        jax.ShapeDtypeStruct((ROWS, HS), BF16),
+        jax.ShapeDtypeStruct((ROWS, HS), BF16),
+        jax.ShapeDtypeStruct((512, HS), BF16),
+    )
+    results = pl.pallas_call(
         kernel,
-        out_shape=(
-            jax.ShapeDtypeStruct((ROWS, 512), BF16),
-            jax.ShapeDtypeStruct((ROWS, HS), BF16),
-            jax.ShapeDtypeStruct((ROWS, HS), BF16),
-            jax.ShapeDtypeStruct((512, HS), BF16),
-        ),
+        out_shape=out_shape,
         in_specs=[pl.BlockSpec(memory_space=pltpu.SMEM)] + [hbm] * 5,
         out_specs=(vmem,) * 4,
         scratch_shapes=scratch,
@@ -579,6 +628,12 @@
         ),
         cost_estimate=pl.CostEstimate(flops=14 * 10**9, bytes_accessed=10**7, transcendentals=4 * 10**6),
     )(passage_lengths, queries, keys, values, grad_out, out_weight)
+    return pl.pallas_call(
+        hand_over,
+        out_shape=out_shape,
+        in_specs=[vmem] * 4,
+        out_specs=(vmem,) * 4,
+    )(*results)
 
 
 def solution(mesh):

time: 109 us -> 95.7 us (0.88)
  the two profiles are of different devices: /device:TPU:192 before, /device:TPU:8 now
where the time goes in v2:
time: 95.7 us; the launch traced here: 95.6 us
  Pallas kernels  95 us (99%)
    pallas_call x1, Pallas kernels, on_device(): pl.pallas_call(kernel, out_shape=out_shape, in_specs=[pl.BlockSpec(memory...  92.6 us
    pallas_call x1, Pallas kernels, on_device(): pl.pallas_call(hand_over, out_shape=out_shape, in_specs=[vmem] * 4, out_s...  2.36 us

profile of v2, /device:TPU:8, one launch (start us, length us, event | category | flops | bytes accessed | tf_op | source)
XLA Modules:
  0.0 95.6 jit_solution(17100281167554132562)
XLA Ops:
  0.6 92.6 %shard_map.93 = (bf16[768,512]{1,0:T(8,128)(2,1)}, bf16[768,128]{1,0:T(8,128)(2,1)}, bf16[768,128]{1,0:T(8,128)(2,1)}, bf16[512,128]{1,0:T(8,128)(2,1)}) custom-call(s32[64]{0:T(128)} %len_ref.1, bf16[768,512]{1,0:T(8,128)(2,1)} %q_hbm.1, bf16[768,128]{1,0:T(8,128)(2,1)} %k_hbm.1, bf16[768,128]{1,0:T(8,128)(2,1)} %v_hbm.1, bf16[768,512]{1,0:T(8,128)(2,1)} %g_hbm.1, ...), custom_call_target="tpu_custom_call" | custom-call | flops 14000000000 | bytes 10000000 | tf_op jit(solution)/shard_map/pallas_call | solution.py:620
  93.2 2.4 %shard_map.94 = (bf16[768,512]{1,0:T(8,128)(2,1)}, bf16[768,128]{1,0:T(8,128)(2,1)}, bf16[768,128]{1,0:T(8,128)(2,1)}, bf16[512,128]{1,0:T(8,128)(2,1)}) custom-call(bf16[768,512]{1,0:T(8,128)(2,1)} %get-tuple-element.8.refs_0_, bf16[768,128]{1,0:T(8,128)(2,1)} %get-tuple-element.9.refs_1_, bf16[768,128]{1,0:T(8,128)(2,1)} %get-tuple-element.10.refs_2_, ...), custom_call_target="tpu_custom_call" | custom-call | tf_op jit(solution)/shard_map/pallas_call | solution.py:631

commit v3 on v2

--- a/solution.py
+++ b/solution.py
@@ -285,10 +285,8 @@
         st0[4 + h : 5 + h, 0:ANS] = jnp.sum(jnp.exp2(sc - top), axis=0, keepdims=True)
 
     share(st0, stz, z_devs, 0)
+    ag_forward(2)
     forward(0)
-    tree_wait(1, leaf)
-    ag_own(STAGES)
-
     def half_of(k, xr, half):
         slot = 2 * ((x + xr + 4 - y) % 4) + (half + c) % 2
         return G[k][slot]
@@ -378,15 +376,22 @@
         else:
             dat[...] = (da[...] + part).astype(BF16)
 
+    ag_done(0)
+    rs_start(0)
+    ag_far(1)
+    ag_forward(3)
+    tree_wait(1, leaf)
+    ag_own(STAGES)
+
     shared(stz, z_devs, 0)
     top, total = merged(st0, stz, 7)
     st1[0:4, :] = top
     st1[4:8, :] = total
     share(st1, stx, x_devs, 1)
-    ag_done(0)
-    rs_start(0)
-    ag_forward(2)
-    ag_far(1)
+    rs_pass(0)
+    ag_done(1)
+    rs_start(1)
+    ag_far(2)
     shared(stx, x_devs, 1)
     top, total = merged(st1, stx, 3)
     for h in range(4):
@@ -397,11 +402,6 @@
     for d in range(3):
         send(oa, oax.at[d], oxs.at[d], oxr.at[d], x_devs[d])
 
-    rs_pass(0)
-    ag_done(1)
-    rs_start(1)
-    ag_forward(3)
-    ag_far(2)
     ag_forward(STAGES)
     lax.fori_loop(4, 8, permute_w, 0)
     ag_far(3)
@@ -437,10 +437,10 @@
     grad_attn(1)
     grad_attn(2)
     grad_attn(3)
+    rs_pass(3)
     shared(sdz, z_devs, 2)
     sd1[...] = sd0[...] + sum(sdz[i] for i in range(7))
     share(sd1, sdx, x_devs, 3)
-    rs_pass(3)
 
     def backward(i):
         u0 = TB * i

time: 95.7 us -> 99.1 us (1.036); the launches traced: 95.6 us -> 97.6 us
  Pallas kernels: 95 us -> 97 us
    pallas_call x1, Pallas kernels: 92.6 us -> 94.6 us  [on_device(): pl.pallas_call(kernel, out_shape=out_shape, in_specs=[pl.BlockSpec(memory...]
where the time goes in v3:
time: 99.1 us; the launch traced here: 97.6 us
  Pallas kernels  97 us (98%)
    pallas_call x1, Pallas kernels, on_device(): pl.pallas_call(kernel, out_shape=out_shape, in_specs=[pl.BlockSpec(memory...  94.6 us
    pallas_call x1, Pallas kernels, on_device(): pl.pallas_call(hand_over, out_shape=out_shape, in_specs=[vmem] * 4, out_s...  2.36 us

profile of v3, /device:TPU:8, one launch (start us, length us, event | category | flops | bytes accessed | tf_op | source)
XLA Modules:
  0.0 97.6 jit_solution(8827727743245403503)
XLA Ops:
  0.6 94.6 %shard_map.93 = (bf16[768,512]{1,0:T(8,128)(2,1)}, bf16[768,128]{1,0:T(8,128)(2,1)}, bf16[768,128]{1,0:T(8,128)(2,1)}, bf16[512,128]{1,0:T(8,128)(2,1)}) custom-call(s32[64]{0:T(128)} %len_ref.1, bf16[768,512]{1,0:T(8,128)(2,1)} %q_hbm.1, bf16[768,128]{1,0:T(8,128)(2,1)} %k_hbm.1, bf16[768,128]{1,0:T(8,128)(2,1)} %v_hbm.1, bf16[768,512]{1,0:T(8,128)(2,1)} %g_hbm.1, ...), custom_call_target="tpu_custom_call" | custom-call | flops 14000000000 | bytes 10000000 | tf_op jit(solution)/shard_map/pallas_call | solution.py:620
  95.3 2.4 %shard_map.94 = (bf16[768,512]{1,0:T(8,128)(2,1)}, bf16[768,128]{1,0:T(8,128)(2,1)}, bf16[768,128]{1,0:T(8,128)(2,1)}, bf16[512,128]{1,0:T(8,128)(2,1)}) custom-call(bf16[768,512]{1,0:T(8,128)(2,1)} %get-tuple-element.8.refs_0_, bf16[768,128]{1,0:T(8,128)(2,1)} %get-tuple-element.9.refs_1_, bf16[768,128]{1,0:T(8,128)(2,1)} %get-tuple-element.10.refs_2_, ...), custom_call_target="tpu_custom_call" | custom-call | tf_op jit(solution)/shard_map/pallas_call | solution.py:631
